TPU v7x, 1024 devices: a whole 4x4x32 slice. The times are simulated.
1024 devices in a mesh: dp: 16 (over x, y), expert: 64 (over z, core).
Axes of the slice: x: 4, y: 4, z: 32, core: 2. Of those that a mesh axis runs over, the one named last changes fastest.
Arguments:
- tokens: bfloat16 [1024, 7168], P('expert', 'dp'), may hold values from -6 to 6
- expert_ids: int32 [1024, 8], P('expert'), may hold values from 0 to 63, all different within a row; in each aligned block of 16 rows (0 to 15, 16 to 31, ...) at most 4 rows name the same one
- gate_weights: float32 [1024, 8], P('expert'), may hold values from 0.05 to 0.5
- response_mask: int32 [1024], P('expert'), may hold values 0 or 1
- cotangent: bfloat16 [1024, 7168], P('expert', 'dp'), may hold values from -6 to 6
- w_gate: bfloat16 [64, 7168, 1024], P('expert', 'dp'), may hold values from -0.0625 to 0.0625
- w_up: bfloat16 [64, 7168, 1024], P('expert', 'dp'), may hold values from -0.0625 to 0.0625
- w_down: bfloat16 [64, 1024, 7168], P('expert', None, 'dp'), may hold values from -0.1875 to 0.1875
- shared_gate: bfloat16 [7168, 2048], P('dp'), may hold values from -0.0625 to 0.0625
- shared_up: bfloat16 [7168, 2048], P('dp'), may hold values from -0.0625 to 0.0625
- shared_down: bfloat16 [2048, 7168], P(None, 'dp'), may hold values from -0.125 to 0.125
Outputs:
- mixed: bfloat16 [1024, 7168], P('expert', 'dp')
- token_grad: bfloat16 [1024, 7168], P('expert', 'dp')
- gate_grad: float32 [1024, 8], P('expert')
Inputs may be any that keep to these rules, and one draw needn't show every extreme that they name: `expert_ids`: each row names 8 different experts; in each aligned block of 16 rows (the rows of one device) no expert is named by more than 4 rows.
All inputs are finite; a program needn't handle non-finite values. No bound on the sum of `response_mask` on one device may be relied on, other than what follows from the above.
Results may differ from a plain program's by a relative error of at most 0.039.
Values may be sent and summed in bfloat16 or wider, within the bound.
A program may use at most 32 MiB of HBM per device.

v0:
```python
import jax
import jax.numpy as jnp
from jax import lax
from jax.sharding import PartitionSpec as P


def silu_pair(gate_part, up_part):
    sigma = jax.nn.sigmoid(gate_part)
    return gate_part * sigma * up_part


def silu_back(grad_hidden, gate_part, up_part):
    sigma = jax.nn.sigmoid(gate_part)
    grad_gate = grad_hidden * up_part * sigma * (1.0 + gate_part * (1.0 - sigma))
    grad_up = grad_hidden * gate_part * sigma
    return (grad_gate.astype(jnp.bfloat16), grad_up.astype(jnp.bfloat16))


def feature_sums(routed, shared):
    return (
        lax.psum_scatter(routed.astype(jnp.bfloat16), "dp", scatter_dimension=4, tiled=True).astype(
            jnp.float32
        ),
        lax.psum_scatter(shared.astype(jnp.bfloat16), "dp", scatter_dimension=4, tiled=True).astype(
            jnp.float32
        ),
    )


def unit_gather(routed, shared):
    return (
        lax.all_gather(routed, "dp", axis=4, tiled=True),
        lax.all_gather(shared, "dp", axis=4, tiled=True),
    )


def move_rows(buffer):
    return lax.all_to_all(buffer, "expert", split_axis=0, concat_axis=0, tiled=True)


def hidden_parts(received, tokens, w_gate, w_up, shared_gate, shared_up):
    gate_part = jnp.einsum("secd,edf->secf", received, w_gate, preferred_element_type=jnp.float32)
    up_part = jnp.einsum("secd,edf->secf", received, w_up, preferred_element_type=jnp.float32)
    shared_gate_part = jnp.dot(tokens, shared_gate, preferred_element_type=jnp.float32)
    shared_up_part = jnp.dot(tokens, shared_up, preferred_element_type=jnp.float32)
    routed = jnp.stack((gate_part, up_part), axis=3)
    shared = jnp.stack((shared_gate_part, shared_up_part), axis=1)[None, None]
    return feature_sums(routed, shared)


def on_device(
    tokens,
    expert_ids,
    gate_weights,
    response_mask,
    cotangent,
    w_gate,
    w_up,
    w_down,
    shared_gate,
    shared_up,
    shared_down,
):
    tok_rows, width = tokens.shape
    top_count = expert_ids.shape[1]
    local_experts = w_gate.shape[0]
    groups = lax.axis_size("expert")
    experts_all = local_experts * groups
    capacity = max(2, 2 * tok_rows * top_count // experts_all)
    slots = experts_all * capacity
    pair_count = tok_rows * top_count
    flat_ids = expert_ids.reshape(pair_count)
    onehot = (flat_ids[:, None] == jnp.arange(experts_all, dtype=jnp.int32)[None, :]).astype(
        jnp.int32
    )
    earlier = jnp.cumsum(onehot, axis=0) - onehot
    target = flat_ids * capacity + jnp.sum(onehot * earlier, axis=1)
    place = (jnp.arange(slots, dtype=jnp.int32)[:, None] == target[None, :]).astype(jnp.bfloat16)
    place_tokens = jnp.sum(place.reshape(slots, tok_rows, top_count), axis=2)
    send = jnp.dot(place_tokens, tokens, preferred_element_type=jnp.float32).astype(jnp.bfloat16)
    received = move_rows(send.reshape(groups, local_experts * capacity, width))
    received = received.reshape(groups, local_experts, capacity, width)
    routed_share, shared_share = hidden_parts(
        received, tokens, w_gate, w_up, shared_gate, shared_up
    )
    hidden_share = silu_pair(routed_share[:, :, :, 0], routed_share[:, :, :, 1]).astype(
        jnp.bfloat16
    )
    shared_hidden_share = silu_pair(shared_share[0, 0, :, 0], shared_share[0, 0, :, 1]).astype(
        jnp.bfloat16
    )
    hidden_full, shared_hidden_full = unit_gather(
        hidden_share[:, :, :, None], shared_hidden_share[None, None, :, None]
    )
    expert_out = jnp.einsum(
        "secf,efd->secd", hidden_full[:, :, :, 0], w_down, preferred_element_type=jnp.float32
    ).astype(jnp.bfloat16)
    shared_out = jnp.dot(
        shared_hidden_full[0, 0, :, 0], shared_down, preferred_element_type=jnp.float32
    )
    returned = move_rows(expert_out.reshape(groups, local_experts * capacity, width)).reshape(
        slots, width
    )
    routed_pairs = returned[target].reshape(tok_rows, top_count, width).astype(jnp.float32)
    mixed = (shared_out + jnp.sum(gate_weights[:, :, None] * routed_pairs, axis=1)).astype(
        jnp.bfloat16
    )
    grad_out = (cotangent.astype(jnp.float32) * response_mask.astype(jnp.float32)[:, None]).astype(
        jnp.bfloat16
    )
    grad_wide = grad_out.astype(jnp.float32)
    gate_partial = jnp.sum(routed_pairs * grad_wide[:, None, :], axis=2)
    gate_grad = lax.psum(gate_partial, "dp")
    pair_grads = (
        (gate_weights[:, :, None] * grad_wide[:, None, :])
        .astype(jnp.bfloat16)
        .reshape(pair_count, width)
    )
    grad_send = jnp.dot(place, pair_grads, preferred_element_type=jnp.float32).astype(jnp.bfloat16)
    grad_received = move_rows(grad_send.reshape(groups, local_experts * capacity, width))
    grad_received = grad_received.reshape(groups, local_experts, capacity, width)
    routed_dh = jnp.einsum(
        "secd,efd->secf", grad_received, w_down, preferred_element_type=jnp.float32
    )
    shared_dh = jnp.einsum("td,fd->tf", grad_out, shared_down, preferred_element_type=jnp.float32)
    routed_saved, shared_saved = hidden_parts(
        received, tokens, w_gate, w_up, shared_gate, shared_up
    )
    routed_grad_share, shared_grad_share = feature_sums(
        routed_dh[:, :, :, None], shared_dh[None, None, :, None]
    )
    grad_gate, grad_up = silu_back(
        routed_grad_share[:, :, :, 0], routed_saved[:, :, :, 0], routed_saved[:, :, :, 1]
    )
    shared_grad_gate, shared_grad_up = silu_back(
        shared_grad_share[0, 0, :, 0], shared_saved[0, 0, :, 0], shared_saved[0, 0, :, 1]
    )
    routed_pack = jnp.stack((grad_gate, grad_up), axis=3)
    shared_pack = jnp.stack((shared_grad_gate, shared_grad_up), axis=1)[None, None]
    routed_full, shared_full = unit_gather(routed_pack, shared_pack)
    row_grad = jnp.einsum(
        "secf,edf->secd", routed_full[:, :, :, 0], w_gate, preferred_element_type=jnp.float32
    )
    row_grad = row_grad + jnp.einsum(
        "secf,edf->secd", routed_full[:, :, :, 1], w_up, preferred_element_type=jnp.float32
    )
    row_grad = row_grad.astype(jnp.bfloat16)
    shared_in = jnp.einsum(
        "tf,df->td", shared_full[0, 0, :, 0], shared_gate, preferred_element_type=jnp.float32
    )
    shared_in = shared_in + jnp.einsum(
        "tf,df->td", shared_full[0, 0, :, 1], shared_up, preferred_element_type=jnp.float32
    )
    back = move_rows(row_grad.reshape(groups, local_experts * capacity, width)).reshape(
        slots, width
    )
    back_pairs = back[target].reshape(tok_rows, top_count, width).astype(jnp.float32)
    token_grad = (shared_in + jnp.sum(back_pairs, axis=1)).astype(jnp.bfloat16)
    return (mixed, token_grad, gate_grad)


def solution(mesh):
    return jax.shard_map(
        on_device,
        mesh=mesh,
        in_specs=(
            P("expert", "dp"),
            P("expert", None),
            P("expert", None),
            P("expert"),
            P("expert", "dp"),
            P("expert", "dp", None),
            P("expert", "dp", None),
            P("expert", None, "dp"),
            P("dp", None),
            P("dp", None),
            P(None, "dp"),
        ),
        out_specs=(P("expert", "dp"), P("expert", "dp"), P("expert", None)),
        check_vma=False,
    )
```

profile of v0, /device:TPU:32, one launch (start us, length us, event | category | flops | bytes accessed | tf_op | source)
XLA Modules:
  0.0 729.4 jit_solution(12586383123674920680)
XLA Ops:
  7.2 0.8 convert_element_type.180
  8.0 0.8 copy.47
  8.8 0.8 copy.48
  9.8 0.2 reduce_window_sum.11
  10.0 0.2 select_reduce_fusion
  10.1 0.8 fusion.49
  10.9 0.3 convolution_convert_fusion.8
  11.4 0.8 reshape.348
  12.2 29.0 %all-to-all-start.2 = ((bf16[64,4,448]{2,1,0:T(4,128)(2,1)}), bf16[64,4,448]{2,1,0:T(4,128)(2,1)S(1)}, u32[]{:S(2)}, u32[]{:S(2)}) async-start(bf16[64,4,448]{2,1,0:T(4,128)(2,1)} %reshape.348), calls=%async_computation.2 | async-start | bytes 524288 | tf_op jit(solution)/shard_map/all_to_all | solution.py:38
  41.4 0.3 convolution_convert_fusion.7
  41.8 0.8 reshape.342
  42.6 40.9 %all-to-all-done.2 = bf16[64,4,448]{2,1,0:T(4,128)(2,1)S(1)} async-done(((bf16[64,4,448]{2,1,0:T(4,128)(2,1)}), bf16[64,4,448]{2,1,0:T(4,128)(2,1)S(1)}, u32[]{:S(2)}, u32[]{:S(2)}) %all-to-all-start.2) | async-done | bytes 229408 | tf_op jit(solution)/shard_map/all_to_all | solution.py:38
  83.5 5.3 all-to-all-start
  88.8 2.4 fusion.5
  91.2 1.6 copy.70
  92.8 1.5 reshape.381
  94.4 36.8 %all-to-all-done = bf16[64,4,448]{2,1,0:T(4,128)(2,1)S(1)} async-done(((bf16[64,4,448]{2,1,0:T(4,128)(2,1)}), bf16[64,4,448]{2,1,0:T(4,128)(2,1)S(1)}, u32[]{:S(2)}, u32[]{:S(2)}) %all-to-all-start) | async-done | bytes 229408 | tf_op jit(solution)/shard_map/all_to_all | solution.py:38
  131.2 1.6 fusion.4
  132.8 0.4 fusion.3
  133.4 2.6 copy.66
  136.0 4.7 reshape.377
  140.7 62.8 %reduce-scatter.19.cloned.1.call-done = bf16[64,256]{1,0:T(8,128)(2,1)} async-done(((bf16[1024,256]{1,0:T(8,128)(2,1)}), bf16[64,256]{1,0:T(8,128)(2,1)}) %reduce-scatter.19.cloned.1.call-update) | async-done | bytes 32784
  203.5 0.9 reshape.382
  204.5 113.6 %reduce-scatter.15.cloned.1.call-done = bf16[64,512]{1,0:T(8,128)(2,1)} async-done(((bf16[1024,512]{1,0:T(8,128)(2,1)}), bf16[64,512]{1,0:T(8,128)(2,1)}) %reduce-scatter.15.cloned.1.call-update) | async-done | bytes 65552
  318.1 1.0 reshape.378
  319.1 0.2 copy.67
  319.4 0.8 copy.59
  320.3 24.1 %all_gather.13 = bf16[64,1,4,1,1024]{0,2,3,1,4:T(4,128)(2,1)S(1)} all-gather(bf16[64,1,4,1,64]{0,2,3,1,4:T(4,128)(2,1)S(1)} %copy.53), channel_id=1, replica_groups=mesh['dp'=16,'expert'=64] {'dp'}, dimensions={4}, use_global_device_ids=true | all-gather | bytes 557056 | tf_op jit(solution)/shard_map/all_gather | solution.py:32
  344.4 0.6 copy.54
  345.1 1.6 convolution_convert_fusion.6
  346.7 0.9 copy.55
  347.6 23.8 %all-to-all-start.1 = ((bf16[64,4,448]{2,1,0:T(4,128)(2,1)}), bf16[64,4,448]{2,1,0:T(4,128)(2,1)}, u32[]{:S(2)}, u32[]{:S(2)}) async-start(bf16[64,4,448]{2,1,0:T(4,128)(2,1)} %copy.55), calls=%async_computation.1 | async-start | bytes 524288 | tf_op jit(solution)/shard_map/all_to_all | solution.py:38
  371.4 0.2 reduce-scatter.17.cloned.1.call-start
  371.6 1.9 fusion.2
  373.5 0.7 copy.68
  374.3 0.9 copy.82
  375.1 1.9 fusion.1
  377.0 1.0 fusion
  378.0 24.7 %all-gather.3.cloned.1.call-done = bf16[64,1,4,2,1024]{0,2,3,1,4:T(4,128)(2,1)} async-done(((bf16[64,1,4,2,64]{0,2,3,1,4:T(4,128)(2,1)}), bf16[64,1,4,2,1024]{0,2,3,1,4:T(4,128)(2,1)}) %all-gather.3.cloned.1.call-update) | async-done | bytes 1048592 | tf_op jit(solution)/shard_map/all_gather | solution.py:32
  402.7 3.2 fusion.52
  405.9 2.3 copy.73
  408.2 0.6 copy.74
  408.8 1.9 fusion.14
  410.7 0.5 fusion.6
  411.2 0.9 copy.62
  412.1 1.5 all-to-all-done.1
  413.6 22.0 %all-to-all-start.3 = ((bf16[64,4,448]{2,1,0:T(4,128)(2,1)}), bf16[64,4,448]{2,1,0:T(4,128)(2,1)S(1)}, u32[]{:S(2)}, u32[]{:S(2)}) async-start(bf16[64,4,448]{2,1,0:T(4,128)(2,1)} %copy.62), calls=%async_computation.3 | async-start | bytes 524288 | tf_op jit(solution)/shard_map/all_to_all | solution.py:38
  435.8 0.7 copy.64
  436.5 1.3 reshape.375
  437.9 77.6 %reduce-scatter.17.cloned.1.call-done = bf16[128,16]{1,0:T(8,128)(2,1)} async-done(((bf16[2048,16]{1,0:T(8,128)(2,1)}), bf16[128,16]{1,0:T(8,128)(2,1)}) %reduce-scatter.17.cloned.1.call-update) | async-done | bytes 4112
  515.5 0.8 reshape_bitcast_fusion
  516.4 112.8 %reduce-scatter.13.cloned.1.call-done = bf16[128,32]{1,0:T(8,128)(2,1)} async-done(((bf16[2048,32]{1,0:T(8,128)(2,1)}), bf16[128,32]{1,0:T(8,128)(2,1)}) %reduce-scatter.13.cloned.1.call-update) | async-done | bytes 8208
  629.2 0.8 reshape.376
  630.1 22.8 %all_gather.12 = bf16[1,1,16,1,2048]{4,2,3,1,0:T(8,128)(2,1)S(1)} all-gather(bf16[1,1,16,1,128]{4,2,3,1,0:T(8,128)(2,1)S(1)} %multiply_convert_fusion.2), channel_id=1, replica_groups=mesh['dp'=16,'expert'=64] {'dp'}, dimensions={4}, use_global_device_ids=true | all-gather | bytes 69632 | tf_op jit(solution)/shard_map/all_gather | solution.py:33
  653.0 21.4 %all-gather = bf16[16,2,2048]{2,0,1:T(8,128)(2,1)S(1)} all-gather(bf16[16,2,128]{2,0,1:T(8,128)(2,1)S(1)} %pad_maximum_fusion.3), channel_id=2, replica_groups=mesh['dp'=16,'expert'=64] {'dp'}, dimensions={2}, use_global_device_ids=true | all-gather | bytes 139264 | tf_op jit(solution)/shard_map/all_gather | solution.py:33
  674.4 0.6 fusion.36
  675.0 1.1 reshape.347
  676.1 0.8 gather_fusion
  676.9 0.1 fusion.21
  677.1 38.6 %psum.7 = f32[16,8]{1,0:T(8,128)S(1)} all-reduce(f32[16,8]{1,0:T(8,128)S(1)} %get-tuple-element.9), channel_id=1, replica_groups=mesh['dp'=16,'expert'=64] {'dp'}, use_global_device_ids=true, to_apply=%region_10.11 | all-reduce | flops 128 | bytes 1024 | tf_op jit(solution)/shard_map/psum | solution.py:113
  715.7 0.7 copy.63
  716.4 2.7 fusion.8
  719.2 0.8 gather_fusion.1
  720.2 2.7 fusion.9
  (49 shorter events, 2.0 us)
Async XLA Ops:
  7.2 369.8 %copy-start = (bf16[448,2048]{1,0:T(8,128)(2,1)S(1)}, bf16[448,2048]{1,0:T(8,128)(2,1)}, u32[]{:S(2)}) copy-start(bf16[448,2048]{1,0:T(8,128)(2,1)} %param.19) | copy-start | bytes 5505028
  7.2 34.2 %copy-start.4 = (bf16[16,448]{1,0:T(8,128)(2,1)S(1)}, bf16[16,448]{1,0:T(8,128)(2,1)}, u32[]{:S(2)}) copy-start(bf16[16,448]{1,0:T(8,128)(2,1)} %param.11) | copy-start | bytes 43012
  12.2 71.3 %all-to-all-start.2 = ((bf16[64,4,448]{2,1,0:T(4,128)(2,1)}), bf16[64,4,448]{2,1,0:T(4,128)(2,1)S(1)}, u32[]{:S(2)}, u32[]{:S(2)}) async-start(bf16[64,4,448]{2,1,0:T(4,128)(2,1)} %reshape.348), calls=%async_computation.2 | async-start | bytes 524288 | tf_op jit(solution)/shard_map/all_to_all | solution.py:38
  83.5 47.7 %all-to-all-start = ((bf16[64,4,448]{2,1,0:T(4,128)(2,1)}), bf16[64,4,448]{2,1,0:T(4,128)(2,1)S(1)}, u32[]{:S(2)}, u32[]{:S(2)}) async-start(bf16[64,4,448]{2,1,0:T(4,128)(2,1)} %reshape.342), calls=%async_computation | async-start | bytes 524288 | tf_op jit(solution)/shard_map/all_to_all | solution.py:38
  88.8 114.7 %reduce-scatter.19.cloned.1.call-start = ((), (), s32[]{:S(2)}) async-start(), calls=%async_computation.12 | async-start | bytes 557056
  94.3 38.5 %copy-start.1 = (bf16[1,448,1024]{2,1,0:T(8,128)(2,1)S(1)}, bf16[1,448,1024]{2,1,0:T(8,128)(2,1)}, u32[]{:S(2)}) copy-start(bf16[1,448,1024]{2,1,0:T(8,128)(2,1)} %param.16) | copy-start | bytes 2752516
  94.3 223.8 %reduce-scatter.15.cloned.1.call-start = ((), (), s32[]{:S(2)}) async-start(), calls=%async_computation.10 | async-start | bytes 1114112
  140.7 262.0 %all-gather.3.cloned.1.call-start = ((), (), s32[]{:S(2)}) async-start(), calls=%async_computation.8 | async-start | bytes 2228224 | tf_op jit(solution)/shard_map/all_gather | solution.py:32
  344.4 27.2 %copy-start.5 = (bf16[16,448]{1,0:T(8,128)(2,1)S(1)}, bf16[16,448]{1,0:T(8,128)(2,1)}, u32[]{:S(2)}) copy-start(bf16[16,448]{1,0:T(8,128)(2,1)} %param.15) | copy-start | bytes 43012
  347.6 66.0 %all-to-all-start.1 = ((bf16[64,4,448]{2,1,0:T(4,128)(2,1)}), bf16[64,4,448]{2,1,0:T(4,128)(2,1)}, u32[]{:S(2)}, u32[]{:S(2)}) async-start(bf16[64,4,448]{2,1,0:T(4,128)(2,1)} %copy.55), calls=%async_computation.1 | async-start | bytes 524288 | tf_op jit(solution)/shard_map/all_to_all | solution.py:38
  371.4 144.2 %reduce-scatter.17.cloned.1.call-start = ((), (), s32[]{:S(2)}) async-start(), calls=%async_computation.11 | async-start | bytes 557056
  408.8 1.9 copy-start.2
  410.7 25.0 %copy-start.3 = (bf16[1,1,16,1,2048]{4,2,3,1,0:T(8,128)(2,1)S(1)}, bf16[1,1,16,1,2048]{4,2,3,1,0:T(8,128)(2,1)}, u32[]{:S(2)}) copy-start(bf16[1,1,16,1,2048]{4,2,3,1,0:T(8,128)(2,1)} %fusion) | copy-start | bytes 196612
  413.6 305.5 %all-to-all-start.3 = ((bf16[64,4,448]{2,1,0:T(4,128)(2,1)}), bf16[64,4,448]{2,1,0:T(4,128)(2,1)S(1)}, u32[]{:S(2)}, u32[]{:S(2)}) async-start(bf16[64,4,448]{2,1,0:T(4,128)(2,1)} %copy.62), calls=%async_computation.3 | async-start | bytes 524288 | tf_op jit(solution)/shard_map/all_to_all | solution.py:38
  435.7 193.5 %reduce-scatter.13.cloned.1.call-start = ((), (), s32[]{:S(2)}) async-start(), calls=%async_computation.9 | async-start | bytes 557056
Sparse Core Ops, SparseCore 0:
  94.8 108.6 reduce-scatter.18
  209.6 108.4 reduce-scatter.14
  322.3 80.3 all-gather.2
  407.8 107.7 reduce-scatter.16
  521.4 107.6 reduce-scatter.12
where the time goes:
time: 731 us; the launch traced here: 729 us
  waiting for transfers between devices  471 us (64%)
  blocking collectives  107 us (15%)
  starting transfers between devices  80.4 us (11%)
  local copies, waits for them, and re-layouts  34.5 us (5%)
  matrix products  19.7 us (3%)
  between operations  14.2 us (2%)
    unnamed x9, waiting for transfers between devices  367 us
    all_to_all x4, starting transfers between devices, move_rows(): lax.all_to_all(buffer, 'expert', split_axis=0, concat_axis=0, tiled=True)  80.1 us
    all_to_all x4, waiting for transfers between devices, move_rows(): lax.all_to_all(buffer, 'expert', split_axis=0, concat_axis=0, tiled=True)  79.2 us
    all_gather x2, blocking collectives, unit_gather(): lax.all_gather(shared, 'dp', axis=4, tiled=True)  44.2 us
    psum x1, blocking collectives, on_device(): gate_grad = lax.psum(gate_partial, 'dp')  38.6 us
    all_gather x1, waiting for transfers between devices, unit_gather(): lax.all_gather(routed, 'dp', axis=4, tiled=True)  24.7 us
    all_gather x1, blocking collectives, unit_gather(): lax.all_gather(routed, 'dp', axis=4, tiled=True)  24.1 us
    unnamed x33, local copies, waits for them, and re-layouts  22.9 us
  transfers between devices with their start and end apart: 9, of which 8 were waited for; matrix products, arithmetic and copies ran while one was open for 6% of the time, Pallas kernels for 0%

commit v1 on v0

v1 whole, which is shorter than its diff:
```python
import functools

import jax
import jax.numpy as jnp
from jax import lax
from jax.experimental import pallas as pl
from jax.experimental.pallas import tpu as pltpu
from jax.sharding import PartitionSpec as P

MESH = pl.DeviceIdType.MESH
BF = jnp.bfloat16
F32 = jnp.float32
NX, NY, NZ = 4, 4, 32
PEERS = NX * NY
CHUNKS = 4
CAP = 4
TOK = 16
TOP = 8
WIDE = 1024
GRAD = 512
META = 384

TREE_LONG = {0: (4, 2, 1), 4: (8, 6, 5, 3), 8: (12, 10, 9, 7), 12: (16, 15, 14, 13, 11)}
TREE_SHORT = {0: (4, 2, 1), 4: (8, 6, 5, 3), 8: (12, 10, 9, 7), 12: (15, 14, 13, 11)}
TREES = (TREE_LONG, TREE_SHORT)
PARENTS = tuple({k: p for p, ch in t.items() for k in ch} for t in TREES)
HOPS = (1, 2, 3, 4)
SLOTS = (
    ((0, 0), (0, 1), (0, 2), (1, 1), (1, 2), (0, 4), (1, 4), (0, 3)),
    ((1, 3), (0, 5), (1, 5), (0, 6), (1, 6), (0, 8), (1, 8), (0, 7)),
    ((1, 7), (0, 9), (1, 9), (0, 10), (1, 10), (0, 12), (1, 12), (0, 11)),
    ((1, 11), (0, 13), (1, 13), (0, 14), (1, 14), (0, 15), (1, 15), (0, 16)),
)
PLACE = {key: (j, i) for j, row in enumerate(SLOTS) for i, key in enumerate(row)}


def flat(key):
    j, i = PLACE[key]
    return j * 8 + i


def dot(a, b):
    return lax.dot_general(a, b, (((1,), (0,)), ((), ())), preferred_element_type=F32)


def dot_t(a, b):
    return lax.dot_general(a, b, (((1,), (1,)), ((), ())), preferred_element_type=F32)


def kernel(
    tokens, ids, weights, mask, cot, wg_hbm, wu_hbm, wd_hbm, sg_hbm, su_hbm, sd_hbm,
    mixed, token_grad, gate_grad,
    wg, wu, wd, sg, su, sd,
    gath, pick, row_w, row_m, part, got, hid, rout, rsib, comb, back_out, back_in,
    s_part, s_got, s_hid, s_out,
    ld_sem, zs, zr, bs, br, rs_s, rs_r, ag_s, ag_r, ro_s, ro_r, rt_s, rt_r,
):
    dp = lax.axis_index("dp")
    ex = lax.axis_index("expert")
    z = ex // 2
    c = ex % 2
    px = dp // NY
    py = dp % NY
    sign = (1 - 2 * c, 2 * c - 1)

    def z_dev(dz):
        return (dp, lax.rem(z + dz + NZ, NZ) * 2 + c)

    sib = (dp, z * 2 + 1 - c)

    def peer(i):
        tx = lax.rem(px + i // NY, NX)
        ty = lax.rem(py + i % NY, NY)
        return tx, ty

    def peer_dev(i):
        tx, ty = peer(i)
        return (tx * NY + ty, ex)

    def remote(src, dst, ss, rs, dev):
        return pltpu.make_async_remote_copy(
            src_ref=src, dst_ref=dst, send_sem=ss, recv_sem=rs, device_id=dev, device_id_type=MESH
        )

    loads = [
        pltpu.make_async_copy(src, dst, ld_sem.at[n])
        for n, (src, dst) in enumerate(
            ((sg_hbm, sg), (su_hbm, su), (sd_hbm, sd), (wg_hbm, wg), (wu_hbm, wu), (wd_hbm, wd))
        )
    ]
    for load in loads:
        load.start()

    barrier = pltpu.get_barrier_semaphore()
    pl.semaphore_signal(barrier, inc=1, device_id=sib, device_id_type=MESH)
    for h in HOPS:
        pl.semaphore_signal(barrier, inc=1, device_id=z_dev(h), device_id_type=MESH)
        pl.semaphore_signal(barrier, inc=1, device_id=z_dev(-h), device_id_type=MESH)

    def greet(i, carry):
        pl.semaphore_signal(barrier, inc=1, device_id=peer_dev(i), device_id_type=MESH)
        return carry

    lax.fori_loop(1, PEERS, greet, 0)

    lane = lax.broadcasted_iota(jnp.int32, (8, 128), 1)
    row = lax.broadcasted_iota(jnp.int32, (8, 128), 0)

    def spread(at):
        return jnp.where(lane == row + at, 1.0, 0.0).astype(BF)

    w_hi = weights[...].astype(BF)
    w_lo = (weights[...] - w_hi.astype(F32)).astype(BF)
    ids_b = ids[...].astype(F32).astype(BF)
    meta = dot(ids_b, spread(64) + spread(72)) + dot(w_hi, spread(80)) + dot(w_lo, spread(88))
    grad = (cot[...].astype(F32) * mask[...].astype(F32)).astype(BF)
    own = gath.at[0, c, 0]
    own[...] = jnp.zeros((TOK, WIDE), BF)
    own[:, 0:448] = tokens[...]
    own[:, META:512] = (own[:, META:512].astype(F32) + meta).astype(BF)
    own[:, GRAD : GRAD + 448] = grad
    rout[...] = jnp.zeros(rout.shape, BF)

    pl.semaphore_wait(barrier, PEERS + 2 * len(HOPS))

    def z_copy(key, child):
        j, i = PLACE[key]
        jj, ii = PLACE[child]
        n = flat(child)
        d, k = child
        return remote(
            gath.at[j, c, i], gath.at[jj, c, ii], zs.at[n], zr.at[n], z_dev(sign[d] * (k - key[1]))
        )

    def forward(d, p):
        for k in TREES[d].get(p, ()):
            z_copy((0, 0) if p == 0 else (d, p), (d, k)).start()

    def arrive(key):
        d, k = key
        p = PARENTS[d][k]
        z_copy((0, 0) if p == 0 else (d, p), key).wait_recv()
        forward(d, k)

    def sib_copy(j):
        return remote(gath.at[j, c], gath.at[j, c], bs.at[j], br.at[j], sib)

    def relay_in(k):
        arrive((0, k))
        arrive((1, k))

    def stage_d(j):
        for d, k in SLOTS[j]:
            if k in (0, 4, 8, 12):
                continue
            arrive((d, k))
        sib_copy(j).start()

    tok_row = lax.broadcasted_iota(jnp.int32, (128, 128), 0)
    tok_lane = lax.broadcasted_iota(jnp.int32, (128, 128), 1)
    lower = jnp.where((tok_lane < tok_row) & (tok_lane // TOK == tok_row // TOK), 1.0, 0.0).astype(BF)
    ones = jnp.ones((128, 128), BF)
    base = (tok_row // TOK) * CAP

    def selector(meta_f, expert, at):
        match = (tok_lane >= 64) & (tok_lane < 72) & (meta_f == expert)
        hit = dot(jnp.where(match, 1.0, 0.0).astype(BF), ones)
        pos = dot(lower, hit.astype(BF))
        here = (hit > 0.5) & (tok_lane.astype(F32) == (base + at).astype(F32) + pos)
        return jnp.where(here, 1.0, 0.0)

    e_own = ex.astype(F32)
    e_sib = (z * 2 + 1 - c).astype(F32)
    lane64 = lax.broadcasted_iota(jnp.int32, (64, 128), 1)

    def rs_copy(j, i):
        tx, ty = peer(i)
        return remote(part.at[j, tx, ty], got.at[j, i - 1], rs_s.at[j], rs_r.at[j], peer_dev(i))

    def stage_p(j):
        sib_copy(j).wait_recv()
        toks_c = gath[j, c].reshape(128, WIDE)
        toks_s = gath[j, 1 - c].reshape(128, WIDE)
        meta_c = toks_c[:, META:512].astype(F32)
        meta_s = toks_s[:, META:512].astype(F32)
        sel_c = selector(meta_c, e_own, 0)
        sel_s = selector(meta_s, e_own, 0)
        pick[j] = (sel_c + selector(meta_c, e_sib, 32)).astype(BF)
        rows_c = dot(sel_c.T[0:32].astype(BF), toks_c)
        rows_s = dot(sel_s.T[0:32].astype(BF), toks_s)
        rows = jnp.concatenate((rows_c, rows_s), axis=0)
        rmeta = rows[:, META:512]
        same = rmeta == e_own
        both = pltpu.roll(rmeta, 112, 1) + pltpu.roll(rmeta, 104, 1)
        w = jnp.sum(jnp.where(same & (lane64 >= 64) & (lane64 < 72), both, 0.0), axis=1, keepdims=True)
        row_w[j] = jnp.broadcast_to(w, (64, 128))
        row_m[j] = jnp.where(same & (lane64 >= 64) & (lane64 < 80), 1.0, 0.0)
        rows = rows.astype(BF)
        x = rows[:, 0:448]
        g = rows[:, GRAD : GRAD + 448]
        for n, val in enumerate((dot(x, wg[...]), dot(x, wu[...]), dot_t(g, wd[...]))):
            val = val.astype(BF).reshape(NX, TOK, 1024)
            for u in range(NY):
                part[j, :, u, :, n * 256 : n * 256 + 256] = val[:, :, u * 256 : u * 256 + 256]

        def send(i, carry):
            rs_copy(j, i).start()
            return carry

        lax.fori_loop(1, PEERS, send, 0)

    def ag_copy(j, i):
        mine = hid.at[j, dp]
        return remote(mine, mine, ag_s.at[j], ag_r.at[j], peer_dev(i))

    def activations(gate, up, dh, scale):
        sig = jax.nn.sigmoid(gate)
        h = (gate * sig * up).astype(BF)
        gh = dh if scale is None else dh * scale
        gg = (gh * up * sig * (1.0 + gate * (1.0 - sig))).astype(BF)
        gu = (gh * gate * sig).astype(BF)
        return h, gg, gu

    lane16 = lax.broadcasted_iota(jnp.int32, (TOK, 128), 1)

    def stage_e(j):
        remote(got.at[j], got.at[j], rs_s.at[j], rs_r.at[j], sib).wait_recv()
        acc = part[j, px, py].astype(F32)
        for i in range(PEERS - 1):
            acc = acc + got[j, i].astype(F32)
        gate, up, dh = acc[:, 0:256], acc[:, 256:512], acc[:, 512:768]
        w = row_w[j, pl.ds(pl.multiple_of(px * TOK, TOK), TOK), :][:, 0:1]
        h, gg, gu = activations(gate, up, dh, w)
        s = jnp.sum(h.astype(F32) * dh, axis=1, keepdims=True)
        s_hi = s.astype(BF).astype(F32)
        tail = jnp.where(lane16 == 0, s_hi, jnp.where(lane16 == 1, s - s_hi, 0.0)).astype(BF)
        hid[j, dp] = jnp.concatenate((h, gg, gu, tail), axis=1)

        def send(i, carry):
            ag_copy(j, i).start()
            return carry

        lax.fori_loop(1, PEERS, send, 0)

    def ro_copy(j):
        return remote(rout.at[j, pl.ds(32, 32)], rsib.at[j], ro_s.at[j], ro_r.at[j], sib)

    def stage_m(j):
        many = hid.at[j, pl.ds(0, PEERS - 1)]
        remote(many, many, ag_s.at[j], ag_r.at[j], sib).wait_recv()

        def full(n):
            return jnp.concatenate(
                [
                    jnp.concatenate(
                        [hid[j, r * NY + u, :, n * 256 : n * 256 + 256] for u in range(NY)], axis=1
                    )
                    for r in range(NX)
                ],
                axis=0,
            )

        eo = dot(full(0), wd[...])
        rg = dot_t(full(1), wg[...]) + dot_t(full(2), wu[...])
        tails = []
        for r in range(NX):
            t = hid[j, r * NY, :, 768:896].astype(F32)
            for u in range(1, NY):
                t = t + hid[j, r * NY + u, :, 768:896].astype(F32)
            tails.append(t)
        s = jnp.sum(jnp.concatenate(tails, axis=0), axis=1, keepdims=True)
        s_hi = s.astype(BF).astype(F32)
        extra = row_m[j] * jnp.where(lane64 < 72, s_hi, s - s_hi)
        rout[j, :, 0:448] = (eo * row_w[j][:, 0:1]).astype(BF)
        rout[j, :, META:512] = (rout[j, :, META:512].astype(F32) + extra).astype(BF)
        rout[j, :, GRAD : GRAD + 448] = rg.astype(BF)
        ro_copy(j).start()

    def back_copy(key):
        d, k = key
        n = flat(key)
        p = PARENTS[d][k]
        return remote(
            back_out.at[n], back_in.at[n], rt_s.at[n], rt_r.at[n], z_dev(-sign[d] * (k - p))
        )

    def stage_c(j):
        ro_copy(j).wait_recv()
        both = jnp.concatenate((rout[j, 0:32], rsib[j]), axis=0)
        out = dot(pick[j][:, 0:64], both).reshape(8, TOK, WIDE)
        for i, (d, k) in enumerate(SLOTS[j]):
            if k not in (0, 4, 8, 12):
                back_out[j * 8 + i] = out[i].astype(BF)
                back_copy((d, k)).start()
            else:
                comb[j * 8 + i] = out[i]

    def children_sum(d, p, total):
        for k in TREES[d].get(p, ()):
            back_copy((d, k)).wait_recv()
            total = total + back_in[flat((d, k))].astype(F32)
        return total

    def relay_out(k):
        for d in (0, 1):
            n = flat((d, k))
            back_out[n] = children_sum(d, k, comb[n]).astype(BF)
            back_copy((d, k)).start()

    def sr_copy(i):
        tx, ty = peer(i)
        return remote(s_part.at[tx * NY + ty], s_got.at[i - 1], rs_s.at[CHUNKS], rs_r.at[CHUNKS], peer_dev(i))

    def sa_copy(i):
        mine = s_hid.at[dp]
        return remote(mine, mine, ag_s.at[CHUNKS], ag_r.at[CHUNKS], peer_dev(i))

    def shared_p():
        for n, (x, w, load, mul) in enumerate(
            (
                (tokens[...], sg, loads[0], dot),
                (tokens[...], su, loads[1], dot),
                (own[:, GRAD : GRAD + 448], sd, loads[2], dot_t),
            )
        ):
            load.wait()
            val = mul(x, w[...]).astype(BF)
            for p in range(PEERS):
                s_part[p, :, n * 128 : n * 128 + 128] = val[:, p * 128 : p * 128 + 128]

        def send(i, carry):
            sr_copy(i).start()
            return carry

        lax.fori_loop(1, PEERS, send, 0)

    def shared_e():
        remote(s_got, s_got, rs_s.at[CHUNKS], rs_r.at[CHUNKS], sib).wait_recv()
        acc = s_part[dp].astype(F32)
        for i in range(PEERS - 1):
            acc = acc + s_got[i].astype(F32)
        h, gg, gu = activations(acc[:, 0:128], acc[:, 128:256], acc[:, 256:384], None)
        s_hid[dp] = jnp.concatenate((h, gg, gu), axis=1)

        def send(i, carry):
            sa_copy(i).start()
            return carry

        lax.fori_loop(1, PEERS, send, 0)

    def shared_m():
        many = s_hid.at[pl.ds(0, PEERS - 1)]
        remote(many, many, ag_s.at[CHUNKS], ag_r.at[CHUNKS], sib).wait_recv()

        def full(n):
            return jnp.concatenate([s_hid[p, :, n * 128 : n * 128 + 128] for p in range(PEERS)], axis=1)

        s_out[0] = dot(full(0), sd[...])
        s_out[1] = dot_t(full(1), sg[...]) + dot_t(full(2), su[...])

    forward(0, 0)
    forward(1, 0)
    shared_p()
    for load in loads[3:]:
        load.wait()
    relay_in(4)
    stage_d(0)
    shared_e()
    stage_p(0)
    relay_in(8)
    stage_d(1)
    stage_e(0)
    stage_p(1)
    relay_in(12)
    stage_d(2)
    shared_m()
    stage_e(1)
    stage_p(2)
    stage_m(0)
    stage_d(3)
    stage_e(2)
    stage_p(3)
    stage_c(0)
    stage_m(1)
    stage_m(2)
    stage_c(1)
    stage_e(3)
    stage_c(2)
    stage_m(3)
    stage_c(3)
    relay_out(12)
    relay_out(8)
    relay_out(4)
    total = children_sum(1, 0, children_sum(0, 0, comb[0]))
    mixed[...] = (s_out[0] + total[:, 0:448]).astype(BF)
    token_grad[...] = (s_out[1] + total[:, GRAD : GRAD + 448]).astype(BF)
    tail = total[:, META:512]
    gate_grad[...] = (pltpu.roll(tail, 64, 1) + pltpu.roll(tail, 56, 1))[:, 0:TOP]

    for j in range(CHUNKS):
        for i, key in enumerate(SLOTS[j]):
            if key != (0, 0):
                n = j * 8 + i
                remote(gath.at[0, c, 0], gath.at[0, c, 0], zs.at[n], zr.at[n], sib).wait_send()
                back_copy(key).wait_send()
        sib_copy(j).wait_send()
        ro_copy(j).wait_send()
        remote(got.at[j], got.at[j], rs_s.at[j], rs_r.at[j], sib).wait_send()
        many = hid.at[j, pl.ds(0, PEERS - 1)]
        remote(many, many, ag_s.at[j], ag_r.at[j], sib).wait_send()
    remote(s_got, s_got, rs_s.at[CHUNKS], rs_r.at[CHUNKS], sib).wait_send()
    many = s_hid.at[pl.ds(0, PEERS - 1)]
    remote(many, many, ag_s.at[CHUNKS], ag_r.at[CHUNKS], sib).wait_send()


def on_device(
    tokens, expert_ids, gate_weights, response_mask, cotangent,
    w_gate, w_up, w_down, shared_gate, shared_up, shared_down,
):
    vmem = pl.BlockSpec(memory_space=pltpu.VMEM)
    hbm = pl.BlockSpec(memory_space=pl.ANY)
    width = tokens.shape[1]
    units, shared_units = w_gate.shape[2], shared_gate.shape[1]
    sem = pltpu.SemaphoreType.DMA
    blocks = CHUNKS * 8
    return pl.pallas_call(
        kernel,
        out_shape=(
            jax.ShapeDtypeStruct((TOK, width), BF),
            jax.ShapeDtypeStruct((TOK, width), BF),
            jax.ShapeDtypeStruct((TOK, TOP), F32),
        ),
        in_specs=[vmem] * 5 + [hbm] * 6,
        out_specs=(vmem, vmem, vmem),
        scratch_shapes=[
            pltpu.VMEM((width, units), BF),
            pltpu.VMEM((width, units), BF),
            pltpu.VMEM((units, width), BF),
            pltpu.VMEM((width, shared_units), BF),
            pltpu.VMEM((width, shared_units), BF),
            pltpu.VMEM((shared_units, width), BF),
            pltpu.VMEM((CHUNKS, 2, 8, TOK, WIDE), BF),
            pltpu.VMEM((CHUNKS, 128, 128), BF),
            pltpu.VMEM((CHUNKS, 64, 128), F32),
            pltpu.VMEM((CHUNKS, 64, 128), F32),
            pltpu.VMEM((CHUNKS, NX, NY, TOK, 768), BF),
            pltpu.VMEM((CHUNKS, PEERS - 1, TOK, 768), BF),
            pltpu.VMEM((CHUNKS, PEERS, TOK, 896), BF),
            pltpu.VMEM((CHUNKS, 64, WIDE), BF),
            pltpu.VMEM((CHUNKS, 32, WIDE), BF),
            pltpu.VMEM((blocks, TOK, WIDE), F32),
            pltpu.VMEM((blocks, TOK, WIDE), BF),
            pltpu.VMEM((blocks, TOK, WIDE), BF),
            pltpu.VMEM((PEERS, TOK, 384), BF),
            pltpu.VMEM((PEERS - 1, TOK, 384), BF),
            pltpu.VMEM((PEERS, TOK, 384), BF),
            pltpu.VMEM((2, TOK, width), F32),
            sem((6,)),
            sem((blocks,)),
            sem((blocks,)),
            sem((CHUNKS,)),
            sem((CHUNKS,)),
            sem((CHUNKS + 1,)),
            sem((CHUNKS + 1,)),
            sem((CHUNKS + 1,)),
            sem((CHUNKS + 1,)),
            sem((CHUNKS,)),
            sem((CHUNKS,)),
            sem((blocks,)),
            sem((blocks,)),
        ],
        compiler_params=pltpu.CompilerParams(
            collective_id=0, has_side_effects=True, vmem_limit_bytes=50 << 20
        ),
    )(
        tokens,
        expert_ids,
        gate_weights,
        response_mask.reshape(TOK, 1),
        cotangent,
        w_gate[0],
        w_up[0],
        w_down[0],
        shared_gate,
        shared_up,
        shared_down,
    )


def solution(mesh):
    return jax.shard_map(
        on_device,
        mesh=mesh,
        in_specs=(
            P("expert", "dp"),
            P("expert", None),
            P("expert", None),
            P("expert"),
            P("expert", "dp"),
            P("expert", "dp", None),
            P("expert", "dp", None),
            P("expert", None, "dp"),
            P("dp", None),
            P("dp", None),
            P(None, "dp"),
        ),
        out_specs=(P("expert", "dp"), P("expert", "dp"), P("expert", None)),
        check_vma=False,
    )
```

time: 731 us -> 128 us (0.18)
  waiting for transfers between devices: 471 us -> 0 us
  Pallas kernels: 0 us -> 118 us
  blocking collectives: 107 us -> 0 us
  starting transfers between devices: 80.4 us -> 0 us
  local copies, waits for them, and re-layouts: 34.5 us -> 9.53 us
  matrix products: 19.7 us -> 0 us
  between operations: 14.2 us -> 0.69 us
    unnamed x9 -> x0, waiting for transfers between devices: 367 us -> none
    pallas_call x0 -> x1, Pallas kernels: none -> 118 us  [on_device(): pl.pallas_call(kernel, out_shape=(jax.ShapeDtypeStruct((TOK, width), BF),...]
    all_to_all x4 -> x0, starting transfers between devices: 80.1 us -> none  [move_rows(): lax.all_to_all(buffer, 'expert', split_axis=0, concat_axis=0, tiled=True)]
    all_to_all x4 -> x0, waiting for transfers between devices: 79.2 us -> none  [move_rows(): lax.all_to_all(buffer, 'expert', split_axis=0, concat_axis=0, tiled=True)]
    all_gather x3 -> x0, blocking collectives: 68.3 us -> none  [the longest x2 44.2 us: unit_gather(): lax.all_gather(shared, 'dp', axis=4, tiled=True)]
    psum x1 -> x0, blocking collectives: 38.6 us -> none  [on_device(): gate_grad = lax.psum(gate_partial, 'dp')]
    all_gather x1 -> x0, waiting for transfers between devices: 24.7 us -> none  [unit_gather(): lax.all_gather(routed, 'dp', axis=4, tiled=True)]
    dot_general x14 -> x0, matrix products: 19.7 us -> none  [the longest x1 2.7 us: on_device(): jnp.einsum('tf,df->td', shared_full[0, 0, :, 1], shared_up, preferred_ele...]
  transfers between devices with their start and end apart: 9 -> 0, of which waited for: 8 -> 0; matrix products, arithmetic and copies ran while one was open for 6% -> 0% of each run, Pallas kernels for 0% -> 0%
where the time goes in v1:
time: 128 us
  Pallas kernels  118 us (92%)
  local copies, waits for them, and re-layouts  9.53 us (7%)
    pallas_call x1, Pallas kernels, on_device(): pl.pallas_call(kernel, out_shape=(jax.ShapeDtypeStruct((TOK, width), BF),...  118 us
    unnamed x14, local copies, waits for them, and re-layouts  8.14 us

profile of v1, /device:TPU:32, one launch (start us, length us, event | category | flops | bytes accessed | tf_op | source)
XLA Modules:
  0.0 128.1 jit_solution(1565847364563017429)
XLA Ops:
  0.6 0.8 copy.15.ids
  1.4 0.8 copy.16.weights
  2.1 0.7 copy.17.mask
  2.9 1.5 %copy.14 = bf16[1,1024,448]{2,1,0:T(8,128)(2,1)S(1)} copy(bf16[1,1024,448]{1,2,0:T(8,128)(2,1)} %param.18) | data formatting | bytes 1835008 | tf_op args[7]
  4.3 0.0 copy-start
  4.4 0.0 copy-start.1
  4.4 0.0 copy-start.2
  4.4 0.0 copy-start.3
  4.4 3.9 %copy.18.sd_hbm = bf16[2048,448]{1,0:T(8,128)(2,1)} copy(bf16[2048,448]{0,1:T(8,128)(2,1)} %param.21) | data formatting | bytes 3670016 | tf_op args[10]
  8.3 0.0 copy-done
  8.3 0.0 copy-done.1
  8.3 0.0 copy-done.2
  8.3 0.0 copy-done.3
  8.3 117.9 %shard_map.130 = (bf16[16,448]{1,0:T(8,128)(2,1)S(1)}, bf16[16,448]{1,0:T(8,128)(2,1)S(1)}, f32[16,8]{1,0:T(8,128)S(1)}) custom-call(bf16[16,448]{1,0:T(8,128)(2,1)S(1)} %copy-done.2, s32[16,8]{1,0:T(8,128)S(1)} %copy.15.ids, f32[16,8]{1,0:T(8,128)S(1)} %copy.16.weights, s32[16,1]{1,0:T(8,128)S(1)} %copy.17.mask, bf16[16,448]{1,0:T(8,128)(2,1)S(1)} %copy-done.3, ...), custom_call_target="tpu_custom_call" | custom-call | tf_op jit(solution)/shard_map/pallas_call | solution.py:426
  126.3 0.7 copy.19
  126.9 0.6 copy.22
  127.5 0.6 copy.23
Async XLA Ops:
  4.3 4.0 %copy-start = (bf16[1,448,1024]{2,1,0:T(8,128)(2,1)S(1)}, bf16[1,448,1024]{2,1,0:T(8,128)(2,1)}, u32[]{:S(2)}) copy-start(bf16[1,448,1024]{2,1,0:T(8,128)(2,1)} %param.16) | copy-start | bytes 2752516
  4.4 4.0 %copy-start.1 = (bf16[1,448,1024]{2,1,0:T(8,128)(2,1)S(1)}, bf16[1,448,1024]{2,1,0:T(8,128)(2,1)}, u32[]{:S(2)}) copy-start(bf16[1,448,1024]{2,1,0:T(8,128)(2,1)} %param.17) | copy-start | bytes 2752516
  4.4 4.0 %copy-start.2 = (bf16[16,448]{1,0:T(8,128)(2,1)S(1)}, bf16[16,448]{1,0:T(8,128)(2,1)}, u32[]{:S(2)}) copy-start(bf16[16,448]{1,0:T(8,128)(2,1)} %tokens.1) | copy-start | bytes 43012
  4.4 4.0 %copy-start.3 = (bf16[16,448]{1,0:T(8,128)(2,1)S(1)}, bf16[16,448]{1,0:T(8,128)(2,1)}, u32[]{:S(2)}) copy-start(bf16[16,448]{1,0:T(8,128)(2,1)} %cot.1) | copy-start | bytes 43012

commit v2 on v1

--- a/solution.py
+++ b/solution.py
@@ -24,6 +24,8 @@
 TREE_SHORT = {0: (4, 2, 1), 4: (8, 6, 5, 3), 8: (12, 10, 9, 7), 12: (15, 14, 13, 11)}
 TREES = (TREE_LONG, TREE_SHORT)
 PARENTS = tuple({k: p for p, ch in t.items() for k in ch} for t in TREES)
+BACKS = TREES
+BACK_PARENTS = tuple({k: p for p, ch in t.items() for k in ch} for t in BACKS)
 HOPS = (1, 2, 3, 4)
 SLOTS = (
     ((0, 0), (0, 1), (0, 2), (1, 1), (1, 2), (0, 4), (1, 4), (0, 3)),
@@ -47,10 +49,14 @@
     return lax.dot_general(a, b, (((1,), (1,)), ((), ())), preferred_element_type=F32)
 
 
+def t_dot(a, b):
+    return lax.dot_general(a, b, (((0,), (0,)), ((), ())), preferred_element_type=F32)
+
+
 def kernel(
-    tokens, ids, weights, mask, cot, wg_hbm, wu_hbm, wd_hbm, sg_hbm, su_hbm, sd_hbm,
-    mixed, token_grad, gate_grad,
-    wg, wu, wd, sg, su, sd,
+    tokens_hbm, ids_hbm, weights_hbm, mask_hbm, cot_hbm, wg_hbm, wu_hbm, wd_hbm, sg_hbm, su_hbm, sd_hbm,
+    results,
+    tokens, ids, weights, mask, cot, wg, wu, wd, sg, su, sd,
     gath, pick, row_w, row_m, part, got, hid, rout, rsib, comb, back_out, back_in,
     s_part, s_got, s_hid, s_out,
     ld_sem, zs, zr, bs, br, rs_s, rs_r, ag_s, ag_r, ro_s, ro_r, rt_s, rt_r,
@@ -85,11 +91,15 @@
     loads = [
         pltpu.make_async_copy(src, dst, ld_sem.at[n])
         for n, (src, dst) in enumerate(
-            ((sg_hbm, sg), (su_hbm, su), (sd_hbm, sd), (wg_hbm, wg), (wu_hbm, wu), (wd_hbm, wd))
+            (
+                (tokens_hbm, tokens), (ids_hbm, ids), (weights_hbm, weights), (mask_hbm, mask), (cot_hbm, cot),
+                (sg_hbm, sg), (su_hbm, su), (sd_hbm, sd), (wg_hbm, wg), (wu_hbm, wu), (wd_hbm, wd),
+            )
         )
     ]
     for load in loads:
         load.start()
+    small, loads = loads[:5], loads[5:]
 
     barrier = pltpu.get_barrier_semaphore()
     pl.semaphore_signal(barrier, inc=1, device_id=sib, device_id_type=MESH)
@@ -109,12 +119,16 @@
     def spread(at):
         return jnp.where(lane == row + at, 1.0, 0.0).astype(BF)
 
+    for load in small:
+        load.wait()
     w_hi = weights[...].astype(BF)
     w_lo = (weights[...] - w_hi.astype(F32)).astype(BF)
     ids_b = ids[...].astype(F32).astype(BF)
-    meta = dot(ids_b, spread(64) + spread(72)) + dot(w_hi, spread(80)) + dot(w_lo, spread(88))
-    grad = (cot[...].astype(F32) * mask[...].astype(F32)).astype(BF)
-    own = gath.at[0, c, 0]
+    meta = t_dot(ids_b, spread(64) + spread(72)) + t_dot(w_hi, spread(80)) + t_dot(w_lo, spread(88))
+    eye = lax.broadcasted_iota(jnp.int32, (TOK, TOK), 0) == lax.broadcasted_iota(jnp.int32, (TOK, TOK), 1)
+    keep = jnp.where(eye, jnp.broadcast_to(mask[...].astype(F32), (TOK, TOK)), 0.0)
+    grad = dot(keep.astype(BF), cot[...]).astype(BF)
+    own = gath.at[PLACE[(0, 0)][0], c, PLACE[(0, 0)][1]]
     own[...] = jnp.zeros((TOK, WIDE), BF)
     own[:, 0:448] = tokens[...]
     own[:, META:512] = (own[:, META:512].astype(F32) + meta).astype(BF)
@@ -198,7 +212,7 @@
         rows = rows.astype(BF)
         x = rows[:, 0:448]
         g = rows[:, GRAD : GRAD + 448]
-        for n, val in enumerate((dot(x, wg[...]), dot(x, wu[...]), dot_t(g, wd[...]))):
+        for n, val in enumerate((dot(x, wg[...]), dot(x, wu[...]), dot(g, wd[...]))):
             val = val.astype(BF).reshape(NX, TOK, 1024)
             for u in range(NY):
                 part[j, :, u, :, n * 256 : n * 256 + 256] = val[:, :, u * 256 : u * 256 + 256]
@@ -260,7 +274,7 @@
                 axis=0,
             )
 
-        eo = dot(full(0), wd[...])
+        eo = dot_t(full(0), wd[...])
         rg = dot_t(full(1), wg[...]) + dot_t(full(2), wu[...])
         tails = []
         for r in range(NX):
@@ -279,7 +293,7 @@
     def back_copy(key):
         d, k = key
         n = flat(key)
-        p = PARENTS[d][k]
+        p = BACK_PARENTS[d][k]
         return remote(
             back_out.at[n], back_in.at[n], rt_s.at[n], rt_r.at[n], z_dev(-sign[d] * (k - p))
         )
@@ -289,14 +303,14 @@
         both = jnp.concatenate((rout[j, 0:32], rsib[j]), axis=0)
         out = dot(pick[j][:, 0:64], both).reshape(8, TOK, WIDE)
         for i, (d, k) in enumerate(SLOTS[j]):
-            if k not in (0, 4, 8, 12):
+            if k not in BACKS[0]:
                 back_out[j * 8 + i] = out[i].astype(BF)
                 back_copy((d, k)).start()
             else:
                 comb[j * 8 + i] = out[i]
 
     def children_sum(d, p, total):
-        for k in TREES[d].get(p, ()):
+        for k in BACKS[d].get(p, ()):
             back_copy((d, k)).wait_recv()
             total = total + back_in[flat((d, k))].astype(F32)
         return total
@@ -320,7 +334,7 @@
             (
                 (tokens[...], sg, loads[0], dot),
                 (tokens[...], su, loads[1], dot),
-                (own[:, GRAD : GRAD + 448], sd, loads[2], dot_t),
+                (own[:, GRAD : GRAD + 448], sd, loads[2], dot),
             )
         ):
             load.wait()
@@ -355,53 +369,53 @@
         def full(n):
             return jnp.concatenate([s_hid[p, :, n * 128 : n * 128 + 128] for p in range(PEERS)], axis=1)
 
-        s_out[0] = dot(full(0), sd[...])
+        s_out[0] = dot_t(full(0), sd[...])
         s_out[1] = dot_t(full(1), sg[...]) + dot_t(full(2), su[...])
 
     forward(0, 0)
     forward(1, 0)
     shared_p()
+    relay_in(4)
+    stage_d(0)
     for load in loads[3:]:
         load.wait()
-    relay_in(4)
-    stage_d(0)
-    shared_e()
     stage_p(0)
     relay_in(8)
     stage_d(1)
+    shared_e()
+    stage_p(1)
     stage_e(0)
-    stage_p(1)
     relay_in(12)
     stage_d(2)
-    shared_m()
+    stage_p(2)
     stage_e(1)
-    stage_p(2)
     stage_m(0)
     stage_d(3)
+    stage_p(3)
+    shared_m()
     stage_e(2)
-    stage_p(3)
     stage_c(0)
     stage_m(1)
+    stage_e(3)
+    stage_c(1)
     stage_m(2)
-    stage_c(1)
-    stage_e(3)
     stage_c(2)
     stage_m(3)
     stage_c(3)
     relay_out(12)
     relay_out(8)
     relay_out(4)
-    total = children_sum(1, 0, children_sum(0, 0, comb[0]))
-    mixed[...] = (s_out[0] + total[:, 0:448]).astype(BF)
-    token_grad[...] = (s_out[1] + total[:, GRAD : GRAD + 448]).astype(BF)
+    total = children_sum(1, 0, children_sum(0, 0, comb[flat((0, 0))]))
+    results[0:TOK] = s_out[0] + total[:, 0:448]
+    results[TOK : 2 * TOK] = s_out[1] + total[:, GRAD : GRAD + 448]
     tail = total[:, META:512]
-    gate_grad[...] = (pltpu.roll(tail, 64, 1) + pltpu.roll(tail, 56, 1))[:, 0:TOP]
+    results[2 * TOK :, 0:TOK] = dot_t(spread(64) + spread(72), tail.astype(BF))
 
     for j in range(CHUNKS):
         for i, key in enumerate(SLOTS[j]):
             if key != (0, 0):
                 n = j * 8 + i
-                remote(gath.at[0, c, 0], gath.at[0, c, 0], zs.at[n], zr.at[n], sib).wait_send()
+                remote(own, own, zs.at[n], zr.at[n], sib).wait_send()
                 back_copy(key).wait_send()
         sib_copy(j).wait_send()
         ro_copy(j).wait_send()
@@ -418,27 +432,28 @@
     w_gate, w_up, w_down, shared_gate, shared_up, shared_down,
 ):
     vmem = pl.BlockSpec(memory_space=pltpu.VMEM)
-    hbm = pl.BlockSpec(memory_space=pl.ANY)
+    hbm = pl.BlockSpec(memory_space=pltpu.HBM)
     width = tokens.shape[1]
     units, shared_units = w_gate.shape[2], shared_gate.shape[1]
     sem = pltpu.SemaphoreType.DMA
     blocks = CHUNKS * 8
-    return pl.pallas_call(
+    results = pl.pallas_call(
         kernel,
-        out_shape=(
-            jax.ShapeDtypeStruct((TOK, width), BF),
-            jax.ShapeDtypeStruct((TOK, width), BF),
-            jax.ShapeDtypeStruct((TOK, TOP), F32),
-        ),
-        in_specs=[vmem] * 5 + [hbm] * 6,
-        out_specs=(vmem, vmem, vmem),
+        out_shape=jax.ShapeDtypeStruct((2 * TOK + TOP, width), F32),
+        in_specs=[hbm] * 11,
+        out_specs=vmem,
         scratch_shapes=[
+            pltpu.VMEM((TOK, width), BF),
+            pltpu.VMEM((TOP, TOK), jnp.int32),
+            pltpu.VMEM((TOP, TOK), F32),
+            pltpu.VMEM((1, TOK), jnp.int32),
+            pltpu.VMEM((TOK, width), BF),
             pltpu.VMEM((width, units), BF),
             pltpu.VMEM((width, units), BF),
-            pltpu.VMEM((units, width), BF),
+            pltpu.VMEM((width, units), BF),
             pltpu.VMEM((width, shared_units), BF),
             pltpu.VMEM((width, shared_units), BF),
-            pltpu.VMEM((shared_units, width), BF),
+            pltpu.VMEM((width, shared_units), BF),
             pltpu.VMEM((CHUNKS, 2, 8, TOK, WIDE), BF),
             pltpu.VMEM((CHUNKS, 128, 128), BF),
             pltpu.VMEM((CHUNKS, 64, 128), F32),
@@ -455,7 +470,7 @@
             pltpu.VMEM((PEERS - 1, TOK, 384), BF),
             pltpu.VMEM((PEERS, TOK, 384), BF),
             pltpu.VMEM((2, TOK, width), F32),
-            sem((6,)),
+            sem((11,)),
             sem((blocks,)),
             sem((blocks,)),
             sem((CHUNKS,)),
@@ -470,21 +485,22 @@
             sem((blocks,)),
         ],
         compiler_params=pltpu.CompilerParams(
-            collective_id=0, has_side_effects=True, vmem_limit_bytes=50 << 20
+            collective_id=0, has_side_effects=True, vmem_limit_bytes=64 << 20
         ),
     )(
         tokens,
-        expert_ids,
-        gate_weights,
-        response_mask.reshape(TOK, 1),
+        expert_ids.T,
+        gate_weights.T,
+        response_mask.reshape(1, TOK),
         cotangent,
         w_gate[0],
         w_up[0],
-        w_down[0],
+        w_down[0].T,
         shared_gate,
         shared_up,
-        shared_down,
+        shared_down.T,
     )
+    return results[0:TOK].astype(BF), results[TOK : 2 * TOK].astype(BF), results[2 * TOK :, 0:TOK].T
 
 
 def solution(mesh):

time: 128 us -> 113 us (0.88)
  the two profiles are of different devices: /device:TPU:32 before, /device:TPU:1 now
where the time goes in v2:
time: 113 us
  Pallas kernels  110 us (97%)
  local copies, waits for them, and re-layouts  1.89 us (2%)
    pallas_call x1, Pallas kernels, on_device(): pl.pallas_call(kernel, out_shape=jax.ShapeDtypeStruct((2 * TOK + TOP, wid...  110 us

profile of v2, /device:TPU:1, one launch (start us, length us, event | category | flops | bytes accessed | tf_op | source)
XLA Modules:
  0.0 112.9 jit_solution(3453651105142946412)
XLA Ops:
  0.6 109.5 %shard_map.130 = f32[40,448]{1,0:T(8,128)} custom-call(bf16[16,448]{1,0:T(8,128)(2,1)} %tokens_hbm.1, s32[8,16]{1,0:T(8,128)} %bitcast.15, f32[8,16]{1,0:T(8,128)} %bitcast.16, s32[1,16]{1,0:T(1,128)} %bitcast.17, bf16[16,448]{1,0:T(8,128)(2,1)} %cot_hbm.1, bf16[448,1024]{1,0:T(8,128)(2,1)} %bitcast.12, bf16[448,1024]{1,0:T(8,128)(2,1)} %bitcast.13, ...), custom_call_target="tpu_custom_call" | custom-call | tf_op jit(solution)/shard_map/pallas_call | solution.py:440
  110.2 1.3 %slice_bitcast_fusion = f32[16,8]{0,1:T(8,128)} fusion(f32[40,448]{1,0:T(8,128)} %shard_map.130), kind=kLoop, calls=%fused_computation | loop fusion | bytes 1024 | tf_op jit(solution)/shard_map/transpose | solution.py:503
  111.4 0.9 convert.4
  112.3 0.6 fusion

commit v3 on v2

--- a/solution.py
+++ b/solution.py
@@ -24,8 +24,7 @@
 TREE_SHORT = {0: (4, 2, 1), 4: (8, 6, 5, 3), 8: (12, 10, 9, 7), 12: (15, 14, 13, 11)}
 TREES = (TREE_LONG, TREE_SHORT)
 PARENTS = tuple({k: p for p, ch in t.items() for k in ch} for t in TREES)
-BACKS = TREES
-BACK_PARENTS = tuple({k: p for p, ch in t.items() for k in ch} for t in BACKS)
+BACKS, BACK_PARENTS = TREES, PARENTS
 HOPS = (1, 2, 3, 4)
 SLOTS = (
     ((0, 0), (0, 1), (0, 2), (1, 1), (1, 2), (0, 4), (1, 4), (0, 3)),
@@ -389,16 +388,16 @@
     stage_d(2)
     stage_p(2)
     stage_e(1)
-    stage_m(0)
     stage_d(3)
     stage_p(3)
-    shared_m()
+    stage_m(0)
     stage_e(2)
     stage_c(0)
+    stage_e(3)
     stage_m(1)
-    stage_e(3)
     stage_c(1)
     stage_m(2)
+    shared_m()
     stage_c(2)
     stage_m(3)
     stage_c(3)

time: 113 us -> 113 us (level)
  no operation moved by 1% of the time
where the time goes in v3:
time: 113 us
  Pallas kernels  109 us (96%)
  local copies, waits for them, and re-layouts  1.89 us (2%)
    pallas_call x1, Pallas kernels, on_device(): pl.pallas_call(kernel, out_shape=jax.ShapeDtypeStruct((2 * TOK + TOP, wid...  109 us

profile of v3, /device:TPU:1, one launch (start us, length us, event | category | flops | bytes accessed | tf_op | source)
XLA Modules:
  0.0 112.7 jit_solution(8422533898876562627)
XLA Ops:
  0.6 109.3 %shard_map.130 = f32[40,448]{1,0:T(8,128)} custom-call(bf16[16,448]{1,0:T(8,128)(2,1)} %tokens_hbm.1, s32[8,16]{1,0:T(8,128)} %bitcast.15, f32[8,16]{1,0:T(8,128)} %bitcast.16, s32[1,16]{1,0:T(1,128)} %bitcast.17, bf16[16,448]{1,0:T(8,128)(2,1)} %cot_hbm.1, bf16[448,1024]{1,0:T(8,128)(2,1)} %bitcast.12, bf16[448,1024]{1,0:T(8,128)(2,1)} %bitcast.13, ...), custom_call_target="tpu_custom_call" | custom-call | tf_op jit(solution)/shard_map/pallas_call | solution.py:439
  109.9 1.3 %slice_bitcast_fusion = f32[16,8]{0,1:T(8,128)} fusion(f32[40,448]{1,0:T(8,128)} %shard_map.130), kind=kLoop, calls=%fused_computation | loop fusion | bytes 1024 | tf_op jit(solution)/shard_map/transpose | solution.py:502
  111.2 0.9 convert.4
  112.1 0.6 fusion
